TPU v7x, 32 devices: a whole 2x2x4 slice. The times are simulated.
32 devices in a mesh: leaf: 16 (over z, x, core), level: 2 (over y).
Axes of the slice: x: 2, y: 2, z: 4, core: 2. Of those that a mesh axis runs over, the one named last changes fastest.
Arguments:
- charges: bfloat16 [384, 128, 256], P(('leaf', 'level')), may hold values from -6 to 6
- near_mat: bfloat16 [384, 16, 128, 128], P(('leaf', 'level')), may hold values from -0.1875 to 0.1875
- near_source: int32 [384, 16], P(('leaf', 'level')), may hold values from 0 to 71
- near_count: int32 [384], P(('leaf', 'level')), may hold values from 1 to 16, as said below
- moment_map: bfloat16 [384, 256, 128], P(('leaf', 'level')), may hold values from -0.109375 to 0.109375
- local_eval: bfloat16 [384, 128, 256], P(('leaf', 'level')), may hold values from -0.375 to 0.375
- upward_child_translation: bfloat16 [8, 256, 256], replicated, may hold values from -0.125 to 0.125
- shift_down: bfloat16 [8, 256, 256], replicated, may hold values from -0.375 to 0.375
- transfer_ops: bfloat16 [8, 256, 256], replicated, may hold values from -0.0625 to 0.0625
- subtree_interaction_list: int32 [16, 32], P('leaf'), may hold values from 0 to 15
- subtree_interaction_operators: int32 [16, 32], P('leaf'), may hold values from 0 to 7
- parent_list: int32 [16, 8], P('leaf'), may hold values from 0 to 1
- parent_ops: int32 [16, 8], P('leaf'), may hold values from 0 to 7
Outputs:
- potential: float32 [384, 128, 256], P(('leaf', 'level'))
Inputs may be any that keep to these rules, and one draw needn't show every extreme that they name: `near_count`: some block uses all 16 slots and some block only one.
All inputs are finite; a program needn't handle non-finite values.
Results may differ from a plain program's by a relative error of at most 0.012.
Values may be sent and summed in bfloat16 or wider, within the bound.
A program may use at most 128 MiB of HBM per device.

v0:
```python
import jax
import jax.numpy as jnp
from jax import lax
from jax.sharding import PartitionSpec as P


def extended_2(cells, sides, width):
    for axis, dim in sides:
        count = lax.axis_size(axis)
        ends = count - 1
        head = lax.slice_in_dim(cells, 0, width, axis=dim)
        tail = lax.slice_in_dim(cells, cells.shape[dim] - width, cells.shape[dim], axis=dim)
        cells = jnp.concatenate(
            [
                lax.ppermute(tail, axis, [(i, (i + 1) % count) for i in range(ends)]),
                cells,
                lax.ppermute(head, axis, [((i + 1) % count, i) for i in range(ends)]),
            ],
            axis=dim,
        )
    return cells


def top_tree(
    every,
    upward_child_translation,
    shift_down,
    transfer_ops,
    subtree_interaction_list,
    subtree_interaction_operators,
    parent_list,
    parent_ops,
    leaf_index,
):
    leaves, coeffs, columns = every.shape
    grouped_terms = every.reshape(leaves // 8, 8, coeffs, columns)
    upper_levels = jnp.einsum(
        "get,kgtv->kev", upward_child_translation, grouped_terms, preferred_element_type=jnp.float32
    ).astype(jnp.bfloat16)
    coarse = jnp.einsum(
        "kcd,kdr->cr",
        transfer_ops[parent_ops[0]],
        upper_levels[parent_list[0]],
        preferred_element_type=jnp.float32,
    ).astype(jnp.bfloat16)
    far_leaf = jnp.einsum(
        "kcd,kdr->cr",
        transfer_ops[subtree_interaction_operators[0]],
        every[subtree_interaction_list[0]],
        preferred_element_type=jnp.float32,
    )
    downward = jnp.dot(shift_down[leaf_index % 8], coarse, preferred_element_type=jnp.float32)
    return (far_leaf + downward).astype(jnp.bfloat16)


def on_device(
    charges,
    near_mat,
    near_source,
    near_count,
    moment_map,
    local_eval,
    upward_child_translation,
    shift_down,
    transfer_ops,
    subtree_interaction_list,
    subtree_interaction_operators,
    parent_list,
    parent_ops,
):
    slots = near_mat.shape[1]
    subtree = lax.all_gather(charges, "level", axis=0, tiled=True)
    extended = extended_2(subtree, (("leaf", 0),), subtree.shape[0])
    picked = extended[near_source]
    active = (jnp.arange(slots, dtype=jnp.int32)[None, :] < near_count[:, None]).astype(
        jnp.bfloat16
    )
    picked = picked * active[:, :, None, None]
    near_part = jnp.einsum("bkpq,bkqr->bpr", near_mat, picked, preferred_element_type=jnp.float32)
    partial_moment = jnp.einsum(
        "bcp,bpr->cr", moment_map, charges, preferred_element_type=jnp.float32
    )
    leaf_index = lax.axis_index("leaf")
    moment = lax.psum_scatter(
        partial_moment.astype(jnp.bfloat16), "level", scatter_dimension=1, tiled=True
    )
    every = lax.all_gather(moment[None], "leaf", axis=0, tiled=True)
    local_part = top_tree(
        every,
        upward_child_translation,
        shift_down,
        transfer_ops,
        subtree_interaction_list,
        subtree_interaction_operators,
        parent_list,
        parent_ops,
        leaf_index,
    )
    local = lax.all_gather(local_part, "level", axis=1, tiled=True)
    far_part = jnp.einsum("bpc,cr->bpr", local_eval, local, preferred_element_type=jnp.float32)
    return near_part + far_part


def solution(mesh):
    placed = (
        P(("leaf", "level"), None, None),
        P(("leaf", "level"), None, None, None),
        P(("leaf", "level"), None),
        P(("leaf", "level")),
        P(("leaf", "level"), None, None),
        P(("leaf", "level"), None, None),
        P(),
        P(),
        P(),
        P("leaf", None),
        P("leaf", None),
        P("leaf", None),
        P("leaf", None),
    )
    return jax.shard_map(
        on_device,
        mesh=mesh,
        in_specs=placed,
        out_specs=P(("leaf", "level"), None, None),
        check_vma=False,
    )
```

profile of v0, /device:TPU:0, one launch (start us, length us, event | category | flops | bytes accessed | tf_op | source)
XLA Modules:
  0.0 168.5 jit_solution(15363044747930083475)
XLA Ops:
  6.5 0.0 copy-start
  6.5 0.0 reduce-scatter.4.cloned.1.call-start
  6.5 1.8 %fusion.5 = bf16[256,256]{1,0:T(8,128)(2,1)S(1)} fusion(bf16[12,256,128]{2,1,0:T(8,128)(2,1)} %param.17, bf16[12,128,256]{2,1,0:T(8,128)(2,1)} %param.13), kind=kOutput, calls=%fused_computation.12 | convolution fusion | flops 201392128 | bytes 1703936 | tf_op jit(solution)/shard_map/bcp,bpr->cr/dot_general | solution.py:80
  8.4 0.8 copy.20
  9.1 0.0 reduce-scatter.4.cloned.1.call-update
  9.2 0.0 all-gather.4.cloned.1.call-start
  9.2 0.7 all-gather.4.cloned.1.call-update
  9.9 0.0 all-gather.6.cloned.1.call-start
  10.0 12.6 %reduce-scatter.4.cloned.1.call-done = bf16[128,256]{1,0:T(8,128)(2,1)} async-done(((bf16[256,256]{1,0:T(8,128)(2,1)}), bf16[128,256]{1,0:T(8,128)(2,1)}) %reduce-scatter.4.cloned.1.call-update) | async-done | bytes 65552
  22.6 1.6 copy.21
  24.1 0.0 all-gather.6.cloned.1.call-update
  24.2 0.7 fusion.16
  24.8 0.0 copy-done
  24.8 0.0 copy-start.4
  24.9 0.0 copy-start.2
  24.9 0.0 copy-start.5
  24.9 0.0 copy-start.6
  24.9 0.0 copy-start.3
  24.9 2.8 %gather_fusion.1 = bf16[32,256,256]{2,1,0:T(8,128)(2,1)} fusion(bf16[8,256,256]{2,1,0:T(8,128)(2,1)S(1)} %copy-done, s32[1024]{0:T(1024)S(1)} %pad_clamp_fusion.3), kind=kCustom, calls=%fused_computation.1 | custom fusion | bytes 8388736 | tf_op jit(solution)/shard_map/gather | solution.py:48
  27.7 0.0 copy-done.4
  27.7 0.6 gather_fusion.3
  28.3 0.0 copy-done.2
  28.3 0.1 reshape.140
  28.4 0.0 copy-done.5
  28.4 0.0 copy-done.6
  28.5 22.9 %all-gather.4.cloned.1.call-done = bf16[24,128,256]{2,1,0:T(8,128)(2,1)} async-done(((bf16[12,128,256]{2,1,0:T(8,128)(2,1)}), bf16[24,128,256]{2,1,0:T(8,128)(2,1)}) %all-gather.4.cloned.1.call-update) | async-done | bytes 1572880 | tf_op jit(solution)/shard_map/all_gather | solution.py:72
  51.4 2.9 %collective-permute-start = (bf16[24,128,256]{2,1,0:T(8,128)(2,1)}, bf16[24,128,256]{2,1,0:T(8,128)(2,1)}, u32[]{:S(2)}, u32[]{:S(2)}) collective-permute-start(bf16[24,128,256]{2,1,0:T(8,128)(2,1)} %all-gather.4.cloned.1.call-done), channel_id=1, source_target_pairs={{0,2},{2,4},{4,6},{6,8},{8,10},{10,12},{12,14},{14,16},{16,18},{18... | collective-permute-start | bytes 4718600 | tf_op jit(solution)/shard_map/ppermute | solution.py:15
  54.2 1.3 collective-permute-start.1
  55.5 0.0 copy-done.3
  55.5 0.1 fusion.15
  55.6 42.9 %all-gather.6.cloned.1.call-done = bf16[4096,128]{1,0:T(8,128)(2,1)} async-done(((bf16[256,128]{1,0:T(8,128)(2,1)}), bf16[4096,128]{1,0:T(8,128)(2,1)}) %all-gather.6.cloned.1.call-update) | async-done | bytes 1048592 | tf_op jit(solution)/shard_map/all_gather | solution.py:87
  98.5 0.0 copy-start.1
  98.5 3.5 %gather_fusion.2 = bf16[32,256,128]{2,1,0:T(8,128)(2,1)} fusion(bf16[16,256,128]{2,1,0:T(8,128)(2,1)} %bitcast.68, s32[1024]{0:T(1024)S(1)} %pad_clamp_fusion.2), kind=kCustom, calls=%fused_computation.2 | custom fusion | bytes 4194432 | tf_op jit(solution)/shard_map/gather | solution.py:49
  102.0 0.0 copy-done.1
  102.0 1.7 %fusion.7 = bf16[2,256,128]{1,2,0:T(8,128)(2,1)S(1)} fusion(bf16[2,8,256,128]{3,2,1,0:T(8,128)(2,1)S(1)} %bitcast.69, bf16[8,256,256]{2,1,0:T(8,128)(2,1)} %param.19), kind=kOutput, calls=%fused_computation.16 | convolution fusion | flops 268500992 | bytes 2228224 | tf_op jit(solution)/shard_map/get,kgtv->kev/dot_general | solution.py:37
  103.7 0.6 gather_fusion.4
  104.3 4.4 %convolution_bitcast_fusion.2 = f32[256,128]{0,1:T(8,128)S(1)} fusion(bf16[32,256,256]{2,1,0:T(8,128)(2,1)} %gather_fusion.1, bf16[32,256,128]{2,1,0:T(8,128)(2,1)} %gather_fusion.2), kind=kOutput, calls=%fused_computation.14 | convolution fusion | flops 536870912 | bytes 6422528 | tf_op jit(solution)/shard_map/kcd,kdr->cr/dot_general | solution.py:46
  108.6 1.5 fusion.9
  110.2 4.9 %all_gather.11 = bf16[256,256]{0,1:T(8,128)(2,1)S(1)} all-gather(bf16[256,128]{0,1:T(8,128)(2,1)S(1)} %fusion.9), channel_id=1, replica_groups=mesh['leaf'=16,'level'=2] {'level'}, dimensions={1}, use_global_device_ids=true | all-gather | bytes 196608 | tf_op jit(solution)/shard_map/all_gather | solution.py:99
  115.1 1.5 fusion.11
  116.7 0.0 collective-permute-done
  116.7 0.0 collective-permute-done.1
  116.7 4.0 %pad_maximum_fusion = bf16[72,128,256]{2,1,0:T(8,128)(2,1)} fusion(bf16[24,128,256]{2,1,0:T(8,128)(2,1)} %collective-permute-done.1, bf16[24,128,256]{2,1,0:T(8,128)(2,1)} %all-gather.4.cloned.1.call-done, bf16[24,128,256]{2,1,0:T(8,128)(2,1)} %collective-permute-done), kind=kLoop, calls=%fused_computation.8 | loop fusion | flops 4718592 | bytes 9437184 | tf_op jit(solution)/shard_map/concatenate | solution.py:13
  120.7 10.6 %gather_fusion = bf16[192,128,256]{2,1,0:T(8,128)(2,1)} fusion(bf16[72,128,256]{2,1,0:T(8,128)(2,1)} %pad_maximum_fusion, s32[1024]{0:T(1024)S(1)} %pad_clamp_fusion.4), kind=kCustom, calls=%fused_computation | custom fusion | bytes 25166592 | tf_op jit(solution)/shard_map/gather | solution.py:74
  131.2 16.7 %copy.16 = bf16[12,16,128,256]{2,3,1,0:T(8,128)(2,1)} copy(bf16[12,16,128,256]{3,2,1,0:T(8,128)(2,1)} %bitcast.67) | data formatting | bytes 25165824 | tf_op jit(solution)/shard_map/gather | solution.py:74
  147.9 11.0 %bitcast_add_fusion = f32[12,128,256]{1,2,0:T(8,128)} fusion(f32[256,12,128]{2,0,1:T(8,128)S(1)} %fusion.11, bf16[12,16,128,128]{3,2,1,0:T(8,128)(2,1)} %param.14, bf16[12,16,128,256]{2,3,1,0:T(8,128)(2,1)} %copy.16, bf16[12,16]{1,0:T(8,128)(2,1)S(1)} %fusion.15), kind=kOutput, calls=%fused_computation.9 | convolution fusion | flops 1617297408 | bytes 22020480 | tf_op jit(solution)/shard_map/bkpq,bkqr->bpr/dot_general | solution.py:79
  159.0 3.0 %copy.17 = f32[12,128,256]{2,1,0:T(8,128)} copy(f32[12,128,256]{1,2,0:T(8,128)} %bitcast_add_fusion) | data formatting | bytes 3145728 | tf_op jit(solution)/shard_map/add | solution.py:101
  (9 shorter events, 0.0 us)
Async XLA Ops:
  6.5 18.3 %copy-start = (bf16[8,256,256]{2,1,0:T(8,128)(2,1)S(1)}, bf16[8,256,256]{2,1,0:T(8,128)(2,1)}, u32[]{:S(2)}) copy-start(bf16[8,256,256]{2,1,0:T(8,128)(2,1)} %param.21) | copy-start | bytes 3145732
  6.5 16.0 %reduce-scatter.4.cloned.1.call-start = ((), (), s32[]{:S(2)}) async-start(), calls=%async_computation.3 | async-start | bytes 196608
  9.2 42.2 %all-gather.4.cloned.1.call-start = ((), (), s32[]{:S(2)}) async-start(), calls=%async_computation.1 | async-start | bytes 2359296 | tf_op jit(solution)/shard_map/all_gather | solution.py:72
  9.9 88.6 %all-gather.6.cloned.1.call-start = ((), (), s32[]{:S(2)}) async-start(), calls=%async_computation.2 | async-start | bytes 1114112 | tf_op jit(solution)/shard_map/all_gather | solution.py:87
  24.8 2.8 %copy-start.4 = (s32[1,8]{1,0:T(1,128)S(1)}, s32[1,8]{1,0:T(1,128)}, u32[]{:S(2)}) copy-start(s32[1,8]{1,0:T(1,128)} %param.25) | copy-start | bytes 100
  24.9 3.5 %copy-start.2 = (s32[12,16]{1,0:T(8,128)S(1)}, s32[12,16]{1,0:T(8,128)}, u32[]{:S(2)}) copy-start(s32[12,16]{1,0:T(8,128)} %param.15) | copy-start | bytes 2308
  24.9 3.5 %copy-start.5 = (s32[1,32]{1,0:T(1,128)S(1)}, s32[1,32]{1,0:T(1,128)}, u32[]{:S(2)}) copy-start(s32[1,32]{1,0:T(1,128)} %param.22) | copy-start | bytes 388
  24.9 3.6 %copy-start.6 = (s32[1,8]{1,0:T(1,128)S(1)}, s32[1,8]{1,0:T(1,128)}, u32[]{:S(2)}) copy-start(s32[1,8]{1,0:T(1,128)} %param.24) | copy-start | bytes 100
  24.9 30.6 %copy-start.3 = (s32[12]{0:T(128)S(1)}, s32[12]{0:T(128)}, u32[]{:S(2)}) copy-start(s32[12]{0:T(128)} %param.16) | copy-start | bytes 148
  51.4 65.3 %collective-permute-start = (bf16[24,128,256]{2,1,0:T(8,128)(2,1)}, bf16[24,128,256]{2,1,0:T(8,128)(2,1)}, u32[]{:S(2)}, u32[]{:S(2)}) collective-permute-start(bf16[24,128,256]{2,1,0:T(8,128)(2,1)} %all-gather.4.cloned.1.call-done), channel_id=1, source_target_pairs={{0,2},{2,4},{4,6},{6,8},{8,10},{10,12},{12,14},{14,16},{16,18},{18... | collective-permute-start | bytes 4718600 | tf_op jit(solution)/shard_map/ppermute | solution.py:15
  54.2 62.4 %collective-permute-start.1 = (bf16[24,128,256]{2,1,0:T(8,128)(2,1)}, bf16[24,128,256]{2,1,0:T(8,128)(2,1)}, u32[]{:S(2)}, u32[]{:S(2)}) collective-permute-start(bf16[24,128,256]{2,1,0:T(8,128)(2,1)} %all-gather.4.cloned.1.call-done), channel_id=1, source_target_pairs={{2,0},{4,2},{6,4},{8,6},{10,8},{12,10},{14,12},{16,14},{18,16},{20... | collective-permute-start | bytes 4718600 | tf_op jit(solution)/shard_map/ppermute | solution.py:17
  98.5 3.5 %copy-start.1 = (bf16[4096,128]{1,0:T(8,128)(2,1)S(1)}, bf16[4096,128]{1,0:T(8,128)(2,1)}, u32[]{:S(2)}) copy-start(bf16[4096,128]{1,0:T(8,128)(2,1)} %all-gather.6.cloned.1.call-done) | copy-start | bytes 3145732
Sparse Core Ops, SparseCore 0:
  9.6 12.9 reduce-scatter.3
  24.1 27.2 all-gather.3
  53.5 44.9 all-gather.5
where the time goes:
time: 169 us
  waiting for transfers between devices  79.1 us (47%)
  local copies, waits for them, and re-layouts  40.2 us (24%)
  matrix products  22 us (13%)
  between operations  13.3 us (8%)
  blocking collectives  4.94 us (3%)
  other arithmetic  4.79 us (3%)
  starting transfers between devices  4.24 us (3%)
    all_gather x1, waiting for transfers between devices, on_device(): every = lax.all_gather(moment[None], 'leaf', axis=0, tiled=True)  42.9 us
    gather x2, local copies, waits for them, and re-layouts, on_device(): picked = extended[near_source]  27.3 us
    all_gather x1, waiting for transfers between devices, on_device(): subtree = lax.all_gather(charges, 'level', axis=0, tiled=True)  22.9 us
    unnamed x4, waiting for transfers between devices  13.3 us
    dot_general x1, matrix products, on_device(): jnp.einsum('bkpq,bkqr->bpr', near_mat, picked, preferred_element_type=jnp...  11 us
    all_gather x1, blocking collectives, on_device(): local = lax.all_gather(local_part, 'level', axis=1, tiled=True)  4.94 us
    dot_general x1, matrix products, top_tree(): jnp.einsum('kcd,kdr->cr', transfer_ops[subtree_interaction_operators[0]],...  4.37 us
    concatenate x1, other arithmetic, extended_2(): jnp.concatenate([lax.ppermute(tail, axis, [(i, (i + 1) % count) for i in...  4 us
  transfers between devices with their start and end apart: 5, of which 3 were waited for; matrix products, arithmetic and copies ran while one was open for 11% of the time, Pallas kernels for 0%

commit v1 on v0

v1 whole, which is shorter than its diff:
```python
import functools

import jax
import jax.numpy as jnp
from jax import lax
from jax.experimental import pallas as pl
from jax.experimental.pallas import tpu as pltpu
from jax.sharding import PartitionSpec as P

MESH = pl.DeviceIdType.MESH
F32 = jnp.float32
BF16 = jnp.bfloat16


def dot(a, b):
    return jnp.dot(a, b, preferred_element_type=F32)


class Plan:
    def __init__(self, n, rows):
        self.count = 0

        def take(k=1):
            first = self.count
            self.count += k
            return first

        self.own_y = [take(n) for _ in range(2)]
        self.own_x = [take() for _ in range(2)]
        self.own_s = take()
        self.mate_x = take(n)
        self.mate_s = [take(n) for _ in range(2)]
        self.outer_y = take(n)
        self.part_y = take(n)
        self.cell_x = take()
        self.cell_z = take(rows)
        self.cell_s = take()
        self.local_y = take(n)


def kernel(
    leaves,
    n,
    plan,
    sources,
    counts,
    cell_list,
    cell_ops,
    up_list,
    up_ops,
    charges,
    near_mat,
    moment_map,
    local_eval,
    upward,
    shift,
    transfer,
    out,
    ext,
    near_v,
    map_v,
    eval_v,
    upward_v,
    shift_v,
    transfer_v,
    part_f,
    part_b,
    part_in,
    every,
    upper,
    local,
    load_sem,
    send_sem,
    recv_sem,
):
    nb, slots = near_mat.shape[0], near_mat.shape[1]
    half = nb // 2
    sub = n * nb
    coeffs = moment_map.shape[1]
    width = part_b.shape[2]
    rows = leaves // 4
    parents = leaves // 8

    leaf = lax.axis_index("leaf")
    level = lax.axis_index("level")
    core = lax.rem(leaf, 2)
    at_x = lax.rem(leaf // 2, 2)
    row = leaf // 4
    sibling = leaf + 1 - 2 * core
    across = leaf + 2 - 4 * at_x
    outer = leaf - 1 + 2 * core
    has_outer = jnp.logical_and(outer >= 0, outer < leaves)

    def mate(d):
        return (leaf, lax.rem(level + d, n))

    def from_level(d):
        return lax.rem(level + n - d, n)

    to_sibling = (sibling, level)
    to_outer = (outer, level)
    to_across = (across, level)

    def to_row(e):
        return (lax.rem(row + e, rows) * 4 + lax.rem(leaf, 4), level)

    def blocks(part, lev, h=None):
        start = (part * n + lev) * nb
        if h is None:
            return ext.at[pl.ds(start, nb)]
        return ext.at[pl.ds(start + h * half, half)]

    def remote(src, dst, to, i):
        return pltpu.make_async_remote_copy(
            src_ref=src,
            dst_ref=dst,
            send_sem=send_sem.at[i],
            recv_sem=recv_sem.at[i],
            device_id=to,
            device_id_type=MESH,
        )

    loads = [
        pltpu.make_async_copy(src, dst, load_sem.at[i])
        for i, (src, dst) in enumerate(
            [
                (charges, blocks(1, level)),
                (moment_map, map_v),
                (upward, upward_v),
                (transfer, transfer_v),
                (shift, shift_v),
                (local_eval, eval_v),
                (near_mat, near_v),
            ]
        )
    ]
    for copy in loads:
        copy.start()

    ext[3 * sub] = jnp.zeros(ext.shape[1:], ext.dtype)

    @pl.when(jnp.logical_not(has_outer))
    def _():
        @pl.loop(0, sub)
        def _(i):
            ext[i] = jnp.zeros(ext.shape[1:], ext.dtype)

    barrier = pltpu.get_barrier_semaphore()
    peers = [mate(d) for d in range(1, n)] + [to_sibling, to_across]
    peers += [to_row(e) for e in range(1, rows)]
    for peer in peers:
        pl.semaphore_signal(barrier, inc=1, device_id=peer, device_id_type=MESH)

    @pl.when(has_outer)
    def _():
        pl.semaphore_signal(barrier, inc=1, device_id=to_outer, device_id_type=MESH)

    pl.semaphore_wait(barrier, len(peers) + has_outer.astype(jnp.int32))

    def own_y(d, h):
        return remote(
            charges.at[pl.ds(h * half, half)], blocks(1, level, h), mate(d), plan.own_y[h] + d
        )

    def own_x(h):
        return remote(
            charges.at[pl.ds(h * half, half)], blocks(0, level, h), to_outer, plan.own_x[h]
        )

    def mate_x(d):
        q = from_level(d)
        return remote(blocks(1, q, 0), blocks(0, q, 0), to_outer, plan.mate_x + d)

    def mate_s(d, h):
        q = from_level(d)
        return remote(blocks(1, q, h), blocks(2, q, h), to_sibling, plan.mate_s[h] + d)

    def outer_y(d):
        return remote(blocks(0, level, 1), blocks(0, level, 1), mate(d), plan.outer_y + d)

    own_s = remote(charges, blocks(2, level), to_sibling, plan.own_s)
    mates = range(1, n)

    for d in mates:
        own_y(d, 0).start()

    @pl.when(has_outer)
    def _():
        own_x(1).start()

    own_s.start()

    loads[0].wait()
    loads[1].wait()
    mine = ext[pl.ds((n + level) * nb, nb)].reshape(nb * ext.shape[1], ext.shape[2])
    maps = jnp.concatenate([map_v[b] for b in range(nb)], axis=1)
    partial = dot(maps, mine)
    for j in range(n):
        piece = partial[:, j * width : (j + 1) * width]
        part_f[j] = piece
        part_b[j] = piece.astype(BF16)

    def part_y(d):
        return remote(part_b.at[lax.rem(level + d, n)], part_in.at[d], mate(d), plan.part_y + d)

    for d in mates:
        part_y(d).start()
    for d in mates:
        own_y(d, 1).start()

    total = part_f[level]
    for d in mates:
        part_y(d).wait_recv()
        total = total + part_in[d].astype(F32)
    every[core, row, at_x] = total.astype(BF16)
    cell = every.at[core, row, at_x]
    cell_x = remote(cell, cell, to_across, plan.cell_x)
    cell_x.start()

    @pl.when(has_outer)
    def _():
        own_x(0).start()

    for d in mates:
        own_y(d, 0).wait_recv()

        @pl.when(has_outer)
        def _():
            mate_x(d).start()

        mate_s(d, 0).start()

    cell_x.wait_recv()

    def cell_z(e):
        pair = every.at[core, row]
        return remote(pair, pair, to_row(e), plan.cell_z + e)

    for e in range(1, rows):
        cell_z(e).start()

    @pl.when(has_outer)
    def _():
        own_x(1).wait_recv()
        for d in mates:
            outer_y(d).start()

    for e in range(1, rows):
        cell_z(e).wait_recv()
    cell_s = remote(every.at[core], every.at[core], to_sibling, plan.cell_s)
    cell_s.start()
    for d in mates:
        own_y(d, 1).wait_recv()
        mate_s(d, 1).start()
    cell_s.wait_recv()

    for copy in loads[2:5]:
        copy.wait()

    def cell_of(i):
        return every[lax.rem(i, 2), i // 4, lax.rem(i // 2, 2)]

    @pl.loop(0, parents)
    def _(p):
        acc = jnp.zeros((coeffs, width), F32)
        for i in range(8):
            acc = acc + dot(upward_v[i], cell_of(p * 8 + i))
        upper[p] = acc.astype(BF16)

    coarse = jnp.zeros((coeffs, width), F32)
    for k in range(up_list.shape[1]):
        coarse = coarse + dot(transfer_v[up_ops[0, k]], upper[up_list[0, k]])
    down = dot(shift_v[lax.rem(leaf, 8)], coarse.astype(BF16))

    def far_step(k, acc):
        for j in range(4):
            i = k * 4 + j
            acc = acc + dot(transfer_v[cell_ops[0, i]], cell_of(cell_list[0, i]))
        return acc

    far = lax.fori_loop(0, cell_list.shape[1] // 4, far_step, down)
    local[level] = far.astype(BF16)

    def local_y(d):
        return remote(local.at[level], local.at[level], mate(d), plan.local_y + d)

    for d in mates:
        local_y(d).start()
    loads[5].wait()
    loads[6].wait()

    own_s.wait_recv()
    for d in mates:
        mate_s(d, 0).wait_recv()
        mate_s(d, 1).wait_recv()

    @pl.when(has_outer)
    def _():
        own_x(0).wait_recv()
        for d in mates:
            mate_x(d).wait_recv()
            outer_y(d).wait_recv()

    for d in mates:
        local_y(d).wait_recv()

    expansion = jnp.concatenate([local[j] for j in range(n)], axis=1)

    @pl.loop(0, nb)
    def _(b):
        acc = dot(eval_v[b], expansion)
        picked = []
        for k in range(slots):
            s = sources[b, k]
            part = (s >= sub).astype(jnp.int32) + (s >= 2 * sub).astype(jnp.int32)
            s = s + core * (2 - 2 * part) * sub
            picked.append(ext[jnp.where(k < counts[b], s, 3 * sub)])
        for k in range(0, slots, 2):
            left = jnp.concatenate([near_v[b, k], near_v[b, k + 1]], axis=1)
            acc = acc + dot(left, jnp.concatenate(picked[k : k + 2], axis=0))
        out[b] = acc

    for d in mates:
        own_y(d, 0).wait_send()
        own_y(d, 1).wait_send()
        part_y(d).wait_send()
        mate_s(d, 0).wait_send()
        mate_s(d, 1).wait_send()
        local_y(d).wait_send()
    own_s.wait_send()
    cell_x.wait_send()
    cell_s.wait_send()
    for e in range(1, rows):
        cell_z(e).wait_send()

    @pl.when(has_outer)
    def _():
        own_x(0).wait_send()
        own_x(1).wait_send()
        for d in mates:
            mate_x(d).wait_send()
            outer_y(d).wait_send()


def on_device(
    leaves,
    n,
    charges,
    near_mat,
    near_source,
    near_count,
    moment_map,
    local_eval,
    upward_child_translation,
    shift_down,
    transfer_ops,
    subtree_interaction_list,
    subtree_interaction_operators,
    parent_list,
    parent_ops,
):
    nb, p_size, cols = charges.shape
    coeffs = moment_map.shape[1]
    width = cols // n
    rows = leaves // 4
    plan = Plan(n, rows)
    smem = pl.BlockSpec(memory_space=pltpu.SMEM)
    hbm = pl.BlockSpec(memory_space=pl.ANY)

    def buf(like):
        return pltpu.VMEM(like.shape, like.dtype)

    return pl.pallas_call(
        functools.partial(kernel, leaves, n, plan),
        out_shape=jax.ShapeDtypeStruct((nb, p_size, cols), F32),
        in_specs=[smem] * 6 + [hbm] * 7,
        out_specs=pl.BlockSpec(memory_space=pltpu.VMEM),
        scratch_shapes=[
            pltpu.VMEM((3 * n * nb + 1, p_size, cols), BF16),
            buf(near_mat),
            buf(moment_map),
            buf(local_eval),
            buf(upward_child_translation),
            buf(shift_down),
            buf(transfer_ops),
            pltpu.VMEM((n, coeffs, width), F32),
            pltpu.VMEM((n, coeffs, width), BF16),
            pltpu.VMEM((n, coeffs, width), BF16),
            pltpu.VMEM((2, rows, 2, coeffs, width), BF16),
            pltpu.VMEM((leaves // 8, coeffs, width), BF16),
            pltpu.VMEM((n, coeffs, width), BF16),
            pltpu.SemaphoreType.DMA((7,)),
            pltpu.SemaphoreType.DMA((plan.count,)),
            pltpu.SemaphoreType.DMA((plan.count,)),
        ],
        compiler_params=pltpu.CompilerParams(
            collective_id=0, has_side_effects=True, vmem_limit_bytes=56 * 2**20
        ),
    )(
        near_source,
        near_count,
        subtree_interaction_list,
        subtree_interaction_operators,
        parent_list,
        parent_ops,
        charges,
        near_mat,
        moment_map,
        local_eval,
        upward_child_translation,
        shift_down,
        transfer_ops,
    )


def solution(mesh):
    split = P(("leaf", "level"))
    placed = (split,) * 6 + (P(),) * 3 + (P("leaf"),) * 4
    return jax.shard_map(
        functools.partial(on_device, mesh.shape["leaf"], mesh.shape["level"]),
        mesh=mesh,
        in_specs=placed,
        out_specs=split,
        check_vma=False,
    )
```

time: 169 us -> 55.2 us (0.33)
  waiting for transfers between devices: 79.1 us -> 0 us
  Pallas kernels: 0 us -> 51.8 us
  local copies, waits for them, and re-layouts: 40.2 us -> 2.65 us
  matrix products: 22 us -> 0 us
  between operations: 13.3 us -> 0.01 us
  blocking collectives: 4.94 us -> 0 us
  other arithmetic: 4.79 us -> 0 us
  starting transfers between devices: 4.24 us -> 0 us
    all_gather x2 -> x0, waiting for transfers between devices: 65.8 us -> none  [the longest x1 42.9 us: on_device(): every = lax.all_gather(moment[None], 'leaf', axis=0, tiled=True)]
    pallas_call x0 -> x1, Pallas kernels: none -> 51.8 us  [on_device(): pl.pallas_call(functools.partial(kernel, leaves, n, plan), out_shape=jax....]
    gather x6 -> x0, local copies, waits for them, and re-layouts: 34.7 us -> none  [the longest x2 27.3 us: on_device(): picked = extended[near_source]]
    dot_general x6 -> x0, matrix products: 22 us -> none  [the longest x1 11 us: on_device(): jnp.einsum('bkpq,bkqr->bpr', near_mat, picked, preferred_element_type=jnp...]
    unnamed x4 -> x0, waiting for transfers between devices: 13.3 us -> none
    all_gather x1 -> x0, blocking collectives: 4.94 us -> none  [on_device(): local = lax.all_gather(local_part, 'level', axis=1, tiled=True)]
    ppermute x2 -> x0, starting transfers between devices: 4.16 us -> none  [the longest x1 2.88 us: extended_2(): lax.ppermute(tail, axis, [(i, (i + 1) % count) for i in range(ends)])]
    concatenate x1 -> x0, other arithmetic: 4 us -> none  [extended_2(): jnp.concatenate([lax.ppermute(tail, axis, [(i, (i + 1) % count) for i in...]
  transfers between devices with their start and end apart: 5 -> 0, of which waited for: 3 -> 0; matrix products, arithmetic and copies ran while one was open for 11% -> 0% of each run, Pallas kernels for 0% -> 0%
where the time goes in v1:
time: 55.2 us; the launch traced here: 54.5 us
  Pallas kernels  51.8 us (94%)
  local copies, waits for them, and re-layouts  2.65 us (5%)
    pallas_call x1, Pallas kernels, on_device(): pl.pallas_call(functools.partial(kernel, leaves, n, plan), out_shape=jax....  51.8 us
    unnamed x1, local copies, waits for them, and re-layouts  2.65 us

profile of v1, /device:TPU:0, one launch (start us, length us, event | category | flops | bytes accessed | tf_op | source)
XLA Modules:
  0.0 54.5 jit_solution(7179913715429185649)
XLA Ops:
  0.0 51.8 %shard_map.127 = f32[12,128,256]{2,1,0:T(8,128)} custom-call(s32[12,16]{1,0:T(8,128)} %sources.1, s32[12]{0:T(128)} %counts.1, s32[1,32]{1,0:T(1,128)} %cell_list.1, s32[1,32]{1,0:T(1,128)} %cell_ops.1, s32[1,8]{1,0:T(1,128)} %up_list.1, s32[1,8]{1,0:T(1,128)} %up_ops.1, bf16[12,128,256]{2,1,0:T(8,128)(2,1)} %charges.1, bf16[12,16,128,128]{3,2,1,0:T(8,128)(2,1)} %near_mat.1, ...), custom_call_target="tpu_custom_call" | custom-call | tf_op jit(solution)/shard_map/pallas_call | solution.py:373
  51.8 2.7 %copy.15 = f32[12,128,256]{2,1,0:T(8,128)} copy(f32[12,128,256]{2,1,0:T(8,128)} %shard_map.127) | data formatting | bytes 3145728

commit v2 on v1

--- a/solution.py
+++ b/solution.py
@@ -16,8 +16,16 @@
     return jnp.dot(a, b, preferred_element_type=F32)
 
 
+def pieces(nb, by_x, cuts_x, cuts_y):
+    def cut(start, stop, cuts):
+        at = [start + (stop - start) * i // cuts for i in range(cuts + 1)]
+        return [(a, b - a) for a, b in zip(at, at[1:]) if b > a]
+
+    return cut(0, by_x, cuts_x), cut(by_x, nb, cuts_y)
+
+
 class Plan:
-    def __init__(self, n, rows):
+    def __init__(self, n, rows, runs):
         self.count = 0
 
         def take(k=1):
@@ -25,12 +33,12 @@
             self.count += k
             return first
 
-        self.own_y = [take(n) for _ in range(2)]
-        self.own_x = [take() for _ in range(2)]
+        self.own_y = {r: take(n) for r in runs}
+        self.own_x = {r: take() for r in runs}
         self.own_s = take()
-        self.mate_x = take(n)
-        self.mate_s = [take(n) for _ in range(2)]
-        self.outer_y = take(n)
+        self.mate_x = {r: take(n) for r in runs}
+        self.mate_s = {r: take(n) for r in runs}
+        self.outer_y = {r: take(n) for r in runs}
         self.part_y = take(n)
         self.cell_x = take()
         self.cell_z = take(rows)
@@ -42,6 +50,8 @@
     leaves,
     n,
     plan,
+    by_x,
+    by_y,
     sources,
     counts,
     cell_list,
@@ -74,7 +84,6 @@
     recv_sem,
 ):
     nb, slots = near_mat.shape[0], near_mat.shape[1]
-    half = nb // 2
     sub = n * nb
     coeffs = moment_map.shape[1]
     width = part_b.shape[2]
@@ -104,11 +113,10 @@
     def to_row(e):
         return (lax.rem(row + e, rows) * 4 + lax.rem(leaf, 4), level)
 
-    def blocks(part, lev, h=None):
+    def blocks(part, lev, run=None):
         start = (part * n + lev) * nb
-        if h is None:
-            return ext.at[pl.ds(start, nb)]
-        return ext.at[pl.ds(start + h * half, half)]
+        first, length = run or (0, nb)
+        return ext.at[pl.ds(start + first, length)]
 
     def remote(src, dst, to, i):
         return pltpu.make_async_remote_copy(
@@ -155,41 +163,6 @@
     def _():
         pl.semaphore_signal(barrier, inc=1, device_id=to_outer, device_id_type=MESH)
 
-    pl.semaphore_wait(barrier, len(peers) + has_outer.astype(jnp.int32))
-
-    def own_y(d, h):
-        return remote(
-            charges.at[pl.ds(h * half, half)], blocks(1, level, h), mate(d), plan.own_y[h] + d
-        )
-
-    def own_x(h):
-        return remote(
-            charges.at[pl.ds(h * half, half)], blocks(0, level, h), to_outer, plan.own_x[h]
-        )
-
-    def mate_x(d):
-        q = from_level(d)
-        return remote(blocks(1, q, 0), blocks(0, q, 0), to_outer, plan.mate_x + d)
-
-    def mate_s(d, h):
-        q = from_level(d)
-        return remote(blocks(1, q, h), blocks(2, q, h), to_sibling, plan.mate_s[h] + d)
-
-    def outer_y(d):
-        return remote(blocks(0, level, 1), blocks(0, level, 1), mate(d), plan.outer_y + d)
-
-    own_s = remote(charges, blocks(2, level), to_sibling, plan.own_s)
-    mates = range(1, n)
-
-    for d in mates:
-        own_y(d, 0).start()
-
-    @pl.when(has_outer)
-    def _():
-        own_x(1).start()
-
-    own_s.start()
-
     loads[0].wait()
     loads[1].wait()
     mine = ext[pl.ds((n + level) * nb, nb)].reshape(nb * ext.shape[1], ext.shape[2])
@@ -200,13 +173,49 @@
         part_f[j] = piece
         part_b[j] = piece.astype(BF16)
 
+    pl.semaphore_wait(barrier, len(peers) + has_outer.astype(jnp.int32))
+
+    def own_y(d, run):
+        return remote(
+            charges.at[pl.ds(*run)], blocks(1, level, run), mate(d), plan.own_y[run] + d
+        )
+
+    def own_x(run):
+        return remote(charges.at[pl.ds(*run)], blocks(0, level, run), to_outer, plan.own_x[run])
+
+    def mate_x(d, run):
+        q = from_level(d)
+        return remote(blocks(1, q, run), blocks(0, q, run), to_outer, plan.mate_x[run] + d)
+
+    def mate_s(d, run):
+        q = from_level(d)
+        return remote(blocks(1, q, run), blocks(2, q, run), to_sibling, plan.mate_s[run] + d)
+
+    def outer_y(d, run):
+        return remote(blocks(0, level, run), blocks(0, level, run), mate(d), plan.outer_y[run] + d)
+
+    own_s = remote(charges, blocks(2, level), to_sibling, plan.own_s)
+    mates = range(1, n)
+
     def part_y(d):
         return remote(part_b.at[lax.rem(level + d, n)], part_in.at[d], mate(d), plan.part_y + d)
 
+    def send_y(runs):
+        for run in runs:
+            for d in mates:
+                own_y(d, run).start()
+
+    def send_x(runs):
+        @pl.when(has_outer)
+        def _():
+            for run in runs:
+                own_x(run).start()
+
     for d in mates:
         part_y(d).start()
-    for d in mates:
-        own_y(d, 1).start()
+    send_y(by_x[:1])
+    send_x(by_y[:1])
+    own_s.start()
 
     total = part_f[level]
     for d in mates:
@@ -216,20 +225,8 @@
     cell = every.at[core, row, at_x]
     cell_x = remote(cell, cell, to_across, plan.cell_x)
     cell_x.start()
-
-    @pl.when(has_outer)
-    def _():
-        own_x(0).start()
-
-    for d in mates:
-        own_y(d, 0).wait_recv()
-
-        @pl.when(has_outer)
-        def _():
-            mate_x(d).start()
-
-        mate_s(d, 0).start()
-
+    send_y(by_x[1:])
+    send_x(by_y[1:])
     cell_x.wait_recv()
 
     def cell_z(e):
@@ -238,20 +235,39 @@
 
     for e in range(1, rows):
         cell_z(e).start()
-
-    @pl.when(has_outer)
-    def _():
-        own_x(1).wait_recv()
-        for d in mates:
-            outer_y(d).start()
+    send_y(by_y)
+
+    def forward_y(runs):
+        @pl.when(has_outer)
+        def _():
+            for run in runs:
+                own_x(run).wait_recv()
+                for d in mates:
+                    outer_y(d, run).start()
+
+    def forward_x(runs):
+        for run in runs:
+            for d in mates:
+                own_y(d, run).wait_recv()
+
+                @pl.when(has_outer)
+                def _():
+                    mate_x(d, run).start()
+
+                mate_s(d, run).start()
+
+    send_x(by_x)
+    forward_x(by_x)
+    forward_y(by_y)
 
     for e in range(1, rows):
         cell_z(e).wait_recv()
     cell_s = remote(every.at[core], every.at[core], to_sibling, plan.cell_s)
     cell_s.start()
-    for d in mates:
-        own_y(d, 1).wait_recv()
-        mate_s(d, 1).start()
+    for run in by_y:
+        for d in mates:
+            own_y(d, run).wait_recv()
+            mate_s(d, run).start()
     cell_s.wait_recv()
 
     for copy in loads[2:5]:
@@ -290,16 +306,19 @@
     loads[6].wait()
 
     own_s.wait_recv()
-    for d in mates:
-        mate_s(d, 0).wait_recv()
-        mate_s(d, 1).wait_recv()
+    for run in by_x + by_y:
+        for d in mates:
+            mate_s(d, run).wait_recv()
 
     @pl.when(has_outer)
     def _():
-        own_x(0).wait_recv()
-        for d in mates:
-            mate_x(d).wait_recv()
-            outer_y(d).wait_recv()
+        for run in by_x:
+            own_x(run).wait_recv()
+            for d in mates:
+                mate_x(d, run).wait_recv()
+        for run in by_y:
+            for d in mates:
+                outer_y(d, run).wait_recv()
 
     for d in mates:
         local_y(d).wait_recv()
@@ -321,12 +340,11 @@
         out[b] = acc
 
     for d in mates:
-        own_y(d, 0).wait_send()
-        own_y(d, 1).wait_send()
         part_y(d).wait_send()
-        mate_s(d, 0).wait_send()
-        mate_s(d, 1).wait_send()
         local_y(d).wait_send()
+        for run in by_x + by_y:
+            own_y(d, run).wait_send()
+            mate_s(d, run).wait_send()
     own_s.wait_send()
     cell_x.wait_send()
     cell_s.wait_send()
@@ -335,11 +353,13 @@
 
     @pl.when(has_outer)
     def _():
-        own_x(0).wait_send()
-        own_x(1).wait_send()
+        for run in by_x + by_y:
+            own_x(run).wait_send()
         for d in mates:
-            mate_x(d).wait_send()
-            outer_y(d).wait_send()
+            for run in by_x:
+                mate_x(d, run).wait_send()
+            for run in by_y:
+                outer_y(d, run).wait_send()
 
 
 def on_device(
@@ -363,7 +383,8 @@
     coeffs = moment_map.shape[1]
     width = cols // n
     rows = leaves // 4
-    plan = Plan(n, rows)
+    by_x, by_y = pieces(nb, nb // 2, 2, 2)
+    plan = Plan(n, rows, by_x + by_y)
     smem = pl.BlockSpec(memory_space=pltpu.SMEM)
     hbm = pl.BlockSpec(memory_space=pl.ANY)
 
@@ -371,7 +392,7 @@
         return pltpu.VMEM(like.shape, like.dtype)
 
     return pl.pallas_call(
-        functools.partial(kernel, leaves, n, plan),
+        functools.partial(kernel, leaves, n, plan, by_x, by_y),
         out_shape=jax.ShapeDtypeStruct((nb, p_size, cols), F32),
         in_specs=[smem] * 6 + [hbm] * 7,
         out_specs=pl.BlockSpec(memory_space=pltpu.VMEM),

time: 55.2 us -> 43.7 us (0.79)
  Pallas kernels: 51.8 us -> 40.6 us
    pallas_call x1, Pallas kernels: 51.8 us -> 40.6 us  [on_device(): pl.pallas_call(functools.partial(kernel, leaves, n, plan, by_x, by_y), ou...]
where the time goes in v2:
time: 43.7 us; the launch traced here: 43.2 us
  Pallas kernels  40.6 us (93%)
  local copies, waits for them, and re-layouts  2.65 us (6%)
    pallas_call x1, Pallas kernels, on_device(): pl.pallas_call(functools.partial(kernel, leaves, n, plan, by_x, by_y), ou...  40.6 us
    unnamed x1, local copies, waits for them, and re-layouts  2.65 us

profile of v2, /device:TPU:0, one launch (start us, length us, event | category | flops | bytes accessed | tf_op | source)
XLA Modules:
  0.0 43.2 jit_solution(3215314698643299867)
XLA Ops:
  0.0 40.6 %shard_map.127 = f32[12,128,256]{2,1,0:T(8,128)} custom-call(s32[12,16]{1,0:T(8,128)} %sources.1, s32[12]{0:T(128)} %counts.1, s32[1,32]{1,0:T(1,128)} %cell_list.1, s32[1,32]{1,0:T(1,128)} %cell_ops.1, s32[1,8]{1,0:T(1,128)} %up_list.1, s32[1,8]{1,0:T(1,128)} %up_ops.1, bf16[12,128,256]{2,1,0:T(8,128)(2,1)} %charges.1, bf16[12,16,128,128]{3,2,1,0:T(8,128)(2,1)} %near_mat.1, ...), custom_call_target="tpu_custom_call" | custom-call | tf_op jit(solution)/shard_map/pallas_call | solution.py:394
  40.6 2.7 %copy.15 = f32[12,128,256]{2,1,0:T(8,128)} copy(f32[12,128,256]{2,1,0:T(8,128)} %shard_map.127) | data formatting | bytes 3145728

commit v3 on v2

--- a/solution.py
+++ b/solution.py
@@ -337,7 +337,7 @@
         for k in range(0, slots, 2):
             left = jnp.concatenate([near_v[b, k], near_v[b, k + 1]], axis=1)
             acc = acc + dot(left, jnp.concatenate(picked[k : k + 2], axis=0))
-        out[b] = acc
+        out[b] = acc.astype(BF16)
 
     for d in mates:
         part_y(d).wait_send()
@@ -393,7 +393,7 @@
 
     return pl.pallas_call(
         functools.partial(kernel, leaves, n, plan, by_x, by_y),
-        out_shape=jax.ShapeDtypeStruct((nb, p_size, cols), F32),
+        out_shape=jax.ShapeDtypeStruct((nb, p_size, cols), BF16),
         in_specs=[smem] * 6 + [hbm] * 7,
         out_specs=pl.BlockSpec(memory_space=pltpu.VMEM),
         scratch_shapes=[
@@ -431,7 +431,7 @@
         upward_child_translation,
         shift_down,
         transfer_ops,
-    )
+    ).astype(F32)
 
 
 def solution(mesh):

time: 43.7 us -> 43.2 us (0.989)
  local copies, waits for them, and re-layouts: 2.65 us -> 0 us
  other arithmetic: 0 us -> 2.43 us
    unnamed x1 -> x0, local copies, waits for them, and re-layouts: 2.65 us -> none
    convert_element_type x0 -> x1, other arithmetic: none -> 2.43 us  [on_device(): return pl.pallas_call(functools.partial(kernel, leaves, n, plan, by_x, by...]
where the time goes in v3:
time: 43.2 us; the launch traced here: 42.7 us
  Pallas kernels  40.3 us (93%)
  other arithmetic  2.43 us (6%)
    pallas_call x1, Pallas kernels, on_device(): pl.pallas_call(functools.partial(kernel, leaves, n, plan, by_x, by_y), ou...  40.3 us
    convert_element_type x1, other arithmetic, on_device(): return pl.pallas_call(functools.partial(kernel, leaves, n, plan, by_x, by...  2.43 us

profile of v3, /device:TPU:0, one launch (start us, length us, event | category | flops | bytes accessed | tf_op | source)
XLA Modules:
  0.0 42.7 jit_solution(4905971651313296914)
XLA Ops:
  0.0 40.3 %shard_map.127 = bf16[12,128,256]{2,1,0:T(8,128)(2,1)} custom-call(s32[12,16]{1,0:T(8,128)} %sources.1, s32[12]{0:T(128)} %counts.1, s32[1,32]{1,0:T(1,128)} %cell_list.1, s32[1,32]{1,0:T(1,128)} %cell_ops.1, s32[1,8]{1,0:T(1,128)} %up_list.1, s32[1,8]{1,0:T(1,128)} %up_ops.1, bf16[12,128,256]{2,1,0:T(8,128)(2,1)} %charges.1, ...), custom_call_target="tpu_custom_call" | custom-call | tf_op jit(solution)/shard_map/pallas_call | solution.py:394
  40.3 2.4 %convert_element_type.3 = f32[12,128,256]{2,1,0:T(8,128)} convert(bf16[12,128,256]{2,1,0:T(8,128)(2,1)} %shard_map.127) | non-fusion elementwise | flops 393216 | bytes 2359296 | tf_op jit(solution)/shard_map/convert_element_type | solution.py:434
